TPU v7x, 32 devices: a whole 2x2x4 slice. The times are simulated.
32 devices in a mesh: groups: 2 (over y), dp: 4 (over z), tensor: 2 (over x), sub: 2 (over core).
Axes of the slice: x: 2, y: 2, z: 4, core: 2. Of those that a mesh axis runs over, the one named last changes fastest.
Arguments:
- val_hidden: bfloat16 [1024, 7168], P(('groups', 'dp', 'sub'), 'tensor'), parts along dimension 0, may hold values from -6 to 6
- val_cotan: bfloat16 [1024, 4096], P(('groups', 'dp', 'sub')), parts along dimension 0, may hold values from -6 to 6
- val_count: int32 [16], P(('groups', 'dp', 'sub')), parts along dimension 0, may hold values from 16 to 64, as said below
- train_hidden: bfloat16 [2048, 7168], P(('groups', 'dp', 'sub'), 'tensor'), parts along dimension 0, may hold values from -6 to 6
- train_cotan: bfloat16 [2048, 4096], P(('groups', 'dp', 'sub')), parts along dimension 0, may hold values from -6 to 6
- seq_len: int32 [32], P('groups'), parts along dimension 0, may hold values from 1 to 64, as said below
- seq_device: int32 [32], P('groups'), parts along dimension 0, may hold values from 0 to 7, as said below
Outputs:
- weighted_grad: bfloat16 [14336, 4096], P(('groups', 'tensor'), ('dp', 'sub')), parts along dimension 0
- seq_weight: float32 [32], P('groups'), parts along dimension 0
There are 2 independent parts, one for each index of `groups`. A program takes and returns all parts, laid end to end along the dimension named above; each array names one. Nothing has to cross between parts.
Inputs may be any that keep to these rules, and one draw needn't show every extreme that they name: `val_count`: the first data device has 16 live slots and the last data device has all 64 slots live. `seq_len`: the sequences of one device fill at most 128 slots; some device holds 2 sequences of length 64. `seq_device`: every data device holds exactly 2 sequences.
All inputs are finite; a program needn't handle non-finite values.
Results may differ from a plain program's by a relative error of at most 0.0046.
The roundings to bfloat16 on the way count: a program that leaves them out, or rounds other values in their place, can miss the bound.
Values may be sent and summed in bfloat16 or wider, within the bound.
A program may use at most 64 MiB of HBM per device.

v0:
```python
import jax
import jax.numpy as jnp
from jax import lax
from jax.sharding import PartitionSpec as P

D = 4096
FF = 7168


def membership(seq_len, seq_device, row_count, capacity):
    seq_order = jnp.arange(seq_len.shape[0], dtype=jnp.int32)
    shared = seq_device[:, None] == seq_device[None, :]
    earlier = seq_order[None, :] < seq_order[:, None]
    offset = jnp.sum(jnp.where(shared & earlier, seq_len[None, :], 0), axis=1)
    row_ids = jnp.arange(row_count, dtype=jnp.int32)
    holder = row_ids // capacity
    within = row_ids % capacity
    inside = (
        (seq_device[None, :] == holder[:, None])
        & (within[:, None] >= offset[None, :])
        & (within[:, None] < (offset + seq_len)[None, :])
    )
    return inside.astype(jnp.float32)


def shards(val_hidden, val_cotan, val_count, train_hidden, train_cotan, seq_len, seq_device):
    contract_rows = (((0,), (0,)), ((), ()))
    val_slots = val_hidden.shape[0]
    val_live = jnp.arange(val_slots, dtype=jnp.int32) < val_count[0]
    val_kept = jnp.where(val_live[:, None], val_hidden, jnp.zeros_like(val_hidden))
    val_columns, train_columns = (
        lax.all_to_all(val_cotan, ("dp", "sub"), split_axis=1, concat_axis=0, tiled=True),
        lax.all_to_all(train_cotan, ("dp", "sub"), split_axis=1, concat_axis=0, tiled=True),
    )
    val_every, train_every = (
        lax.all_gather(val_kept, ("dp", "sub"), axis=0, tiled=True),
        lax.all_gather(train_hidden, ("dp", "sub"), axis=0, tiled=True),
    )
    val_block = lax.dot_general(
        val_every, val_columns, contract_rows, preferred_element_type=jnp.float32
    )
    val_grad = val_block.astype(jnp.bfloat16)
    projected = jnp.dot(train_every, val_grad, preferred_element_type=jnp.float32)
    token_part = jnp.sum(projected * train_columns, axis=1)
    member = membership(seq_len, seq_device, train_every.shape[0], train_hidden.shape[0])
    part_align = jnp.dot(token_part, member, precision=lax.Precision.HIGHEST)
    count_local = val_count[0].astype(jnp.float32)
    val_total = lax.psum(count_local, ("dp", "sub"))
    align = lax.psum(part_align, ("dp", "tensor", "sub"))
    lengths = seq_len.astype(jnp.float32)
    score = align / jnp.sqrt(val_total * lengths * float(FF) * float(D))
    seq_weight = jax.nn.sigmoid(score)
    mass = jnp.sum(seq_weight * lengths)
    row_weight = jnp.dot(member, seq_weight, precision=lax.Precision.HIGHEST)
    weighted_cotan = (row_weight[:, None] * train_columns).astype(jnp.bfloat16)
    weighted = lax.dot_general(
        train_every, weighted_cotan, contract_rows, preferred_element_type=jnp.float32
    )
    weighted_grad = (weighted / jnp.sqrt(mass)).astype(jnp.bfloat16)
    return (weighted_grad, seq_weight)


def solution(mesh):
    return jax.shard_map(
        shards,
        mesh=mesh,
        in_specs=(
            P(("groups", "dp", "sub"), "tensor"),
            P(("groups", "dp", "sub"), None),
            P(("groups", "dp", "sub")),
            P(("groups", "dp", "sub"), "tensor"),
            P(("groups", "dp", "sub"), None),
            P("groups"),
            P("groups"),
        ),
        out_specs=(P(("groups", "tensor"), ("dp", "sub")), P("groups")),
        check_vma=False,
    )
```

profile of v0, /device:TPU:0, one launch (start us, length us, event | category | flops | bytes accessed | tf_op | source)
XLA Modules:
  0.0 231.7 jit_solution(12047744341904695969)
XLA Ops:
  7.2 0.0 copy-start
  7.2 0.0 all-gather.3.cloned.1.call-start
  7.9 1.9 broadcast_select_fusion
  9.8 0.0 all-gather.3.cloned.1.call-update
  9.8 0.0 copy-start.1
  9.9 0.0 copy-start.2
  9.9 0.0 all-gather.5.cloned.1.call-start
  9.9 0.7 all-gather.5.cloned.1.call-update
  10.6 2.3 copy.22
  12.9 6.3 %all-to-all-start.1 = ((bf16[128,8,512]{0,2,1:T(8,128)(2,1)}), bf16[128,8,512]{0,2,1:T(8,128)(2,1)S(1)}, u32[]{:S(2)}, u32[]{:S(2)}) async-start(bf16[128,8,512]{0,2,1:T(8,128)(2,1)} %bitcast.4), calls=%async_computation.1 | async-start | bytes 2097152 | tf_op jit(solution)/shard_map/all_to_all | solution.py:33
  19.2 0.0 copy-done
  19.2 0.8 copy.28
  20.1 51.4 %all-to-all-done.1 = bf16[128,8,512]{0,2,1:T(8,128)(2,1)S(1)} async-done(((bf16[128,8,512]{0,2,1:T(8,128)(2,1)}), bf16[128,8,512]{0,2,1:T(8,128)(2,1)S(1)}, u32[]{:S(2)}, u32[]{:S(2)}) %all-to-all-start.1) | async-done | bytes 1048608 | tf_op jit(solution)/shard_map/all_to_all | solution.py:33
  71.5 3.5 %all-to-all-start = ((bf16[64,8,512]{2,0,1:T(8,128)(2,1)}), bf16[64,8,512]{2,0,1:T(8,128)(2,1)S(1)}, u32[]{:S(2)}, u32[]{:S(2)}) async-start(bf16[64,8,512]{2,0,1:T(8,128)(2,1)} %bitcast.29), calls=%async_computation | async-start | bytes 1048576 | tf_op jit(solution)/shard_map/all_to_all | solution.py:32
  75.0 0.0 copy-done.1
  75.0 0.0 copy-done.2
  75.0 0.2 select_reduce_fusion
  75.2 1.5 convert_bitcast_fusion
  76.7 1.9 copy.23
  78.6 1.8 copy.24
  80.4 13.4 %all-to-all-done = bf16[64,8,512]{2,0,1:T(8,128)(2,1)S(1)} async-done(((bf16[64,8,512]{2,0,1:T(8,128)(2,1)}), bf16[64,8,512]{2,0,1:T(8,128)(2,1)S(1)}, u32[]{:S(2)}, u32[]{:S(2)}) %all-to-all-start) | async-done | bytes 524320 | tf_op jit(solution)/shard_map/all_to_all | solution.py:32
  93.8 57.7 %all-gather.5.cloned.1.call-done = bf16[1024,3584]{1,0:T(8,128)(2,1)} async-done(((bf16[128,3584]{1,0:T(8,128)(2,1)}), bf16[1024,3584]{1,0:T(8,128)(2,1)}) %all-gather.5.cloned.1.call-update) | async-done | bytes 7340048 | tf_op jit(solution)/shard_map/all_gather | solution.py:37
  151.4 10.6 %fusion.1 = f32[1024]{0:T(1024)S(1)} fusion(f32[1024,512]{0,1:T(8,128)} %copy.24, bf16[1024,3584]{1,0:T(8,128)(2,1)} %all-gather.5.cloned.1.call-done, bf16[512,3584]{1,0:T(8,128)(2,1)} %all-gather.3.cloned.1.call-done, bf16[512,512]{1,0:T(8,128)(2,1)S(1)} %bitcast.35), kind=kOutput, calls=%fused_computation.4 | convolution fusion | flops 5640027136 | bytes 13635584 | tf_op jit(solution)/shard_map/dot_general | solution.py:43
  162.1 0.5 convolution_bitcast_fusion
  162.6 15.1 %psum.15 = f32[]{:T(128)} all-reduce(f32[]{:T(128)S(6)} %convert_element_type.33), channel_id=1, replica_groups=mesh['groups'=2,'dp'=4,'tensor'=2,'sub'=2] {'dp','sub'}, use_global_device_ids=true, to_apply=%region_3.4 | all-reduce | flops 1 | bytes 8 | tf_op jit(solution)/shard_map/psum | solution.py:48
  177.7 29.9 %psum.14 = f32[16]{0:T(128)S(1)} all-reduce(f32[16]{0:T(128)S(1)} %convolution_bitcast_fusion), channel_id=1, replica_groups=mesh['groups'=2,'dp'=4,'tensor'=2,'sub'=2] {'dp','tensor','sub'}, use_global_device_ids=true, to_apply=%region_2.3 | all-reduce | flops 16 | bytes 128 | tf_op jit(solution)/shard_map/psum | solution.py:49
  207.6 1.3 multiply_reduce_fusion
  208.9 0.0 copy-start.3
  209.6 0.6 fusion.3
  210.2 8.8 %fusion = bf16[3584,512]{0,1:T(8,128)(2,1)} fusion(bf16[1024,3584]{1,0:T(8,128)(2,1)} %all-gather.5.cloned.1.call-done, f32[]{:T(128)S(6)} %sqrt.7, f32[1024,512]{1,0:T(8,128)S(1)} %bitcast.33, f32[1024]{0:T(1024)S(1)} %bitcast.36), kind=kOutput, calls=%fused_computation.2 | convolution fusion | flops 3762814976 | bytes 13111300 | tf_op jit(solution)/shard_map/dot_general | solution.py:56
  219.0 0.0 copy-done.3
  219.0 5.9 %copy.25 = bf16[3584,512]{1,0:T(8,128)(2,1)} copy(bf16[3584,512]{0,1:T(8,128)(2,1)} %fusion) | data formatting | bytes 7340032
  (4 shorter events, 0.0 us)
Async XLA Ops:
  7.2 12.0 %copy-start = (bf16[64,4096]{1,0:T(8,128)(2,1)S(1)}, bf16[64,4096]{1,0:T(8,128)(2,1)}, u32[]{:S(2)}) copy-start(bf16[64,4096]{1,0:T(8,128)(2,1)} %param.8) | copy-start | bytes 1572868
  7.2 86.6 %all-gather.3.cloned.1.call-start = ((), (), s32[]{:S(2)}) async-start(), calls=%async_computation.2 | async-start | bytes 4128768 | tf_op jit(solution)/shard_map/all_gather | solution.py:36
  9.8 65.2 %copy-start.1 = (s32[16]{0:T(128)S(1)}, s32[16]{0:T(128)}, u32[]{:S(2)}) copy-start(s32[16]{0:T(128)} %param.12) | copy-start | bytes 196
  9.9 65.2 %copy-start.2 = (s32[16]{0:T(128)S(1)}, s32[16]{0:T(128)}, u32[]{:S(2)}) copy-start(s32[16]{0:T(128)} %param.13) | copy-start | bytes 196
  9.9 141.6 %all-gather.5.cloned.1.call-start = ((), (), s32[]{:S(2)}) async-start(), calls=%async_computation.3 | async-start | bytes 8257536 | tf_op jit(solution)/shard_map/all_gather | solution.py:37
  12.9 58.6 %all-to-all-start.1 = ((bf16[128,8,512]{0,2,1:T(8,128)(2,1)}), bf16[128,8,512]{0,2,1:T(8,128)(2,1)S(1)}, u32[]{:S(2)}, u32[]{:S(2)}) async-start(bf16[128,8,512]{0,2,1:T(8,128)(2,1)} %bitcast.4), calls=%async_computation.1 | async-start | bytes 2097152 | tf_op jit(solution)/shard_map/all_to_all | solution.py:33
  71.5 22.3 %all-to-all-start = ((bf16[64,8,512]{2,0,1:T(8,128)(2,1)}), bf16[64,8,512]{2,0,1:T(8,128)(2,1)S(1)}, u32[]{:S(2)}, u32[]{:S(2)}) async-start(bf16[64,8,512]{2,0,1:T(8,128)(2,1)} %bitcast.29), calls=%async_computation | async-start | bytes 1048576 | tf_op jit(solution)/shard_map/all_to_all | solution.py:32
  208.9 10.1 %copy-start.3 = (f32[16]{0:T(128)}, f32[16]{0:T(128)S(1)}, u32[]{:S(2)}) copy-start(f32[16]{0:T(128)S(1)} %get-tuple-element.13) | copy-start | bytes 196
Sparse Core Ops, SparseCore 0:
  10.0 66.9 all-gather.2
  78.6 72.7 all-gather.4
where the time goes:
time: 232 us
  waiting for transfers between devices  123 us (53%)
  blocking collectives  45 us (19%)
  matrix products  20.5 us (9%)
  between operations  15.5 us (7%)
  local copies, waits for them, and re-layouts  12.8 us (6%)
  starting transfers between devices  9.9 us (4%)
  other arithmetic  4.81 us (2%)
    all_gather x1, waiting for transfers between devices, shards(): lax.all_gather(train_hidden, ('dp', 'sub'), axis=0, tiled=True)  57.7 us
    all_to_all x1, waiting for transfers between devices, shards(): lax.all_to_all(train_cotan, ('dp', 'sub'), split_axis=1, concat_axis=0, t...  51.4 us
    psum x1, blocking collectives, shards(): align = lax.psum(part_align, ('dp', 'tensor', 'sub'))  29.9 us
    psum x1, blocking collectives, shards(): val_total = lax.psum(count_local, ('dp', 'sub'))  15.1 us
    all_to_all x1, waiting for transfers between devices, shards(): lax.all_to_all(val_cotan, ('dp', 'sub'), split_axis=1, concat_axis=0, til...  13.4 us
    dot_general x1, matrix products, shards(): jnp.dot(train_every, val_grad, preferred_element_type=jnp.float32)  10.6 us
    dot_general x1, matrix products, shards(): lax.dot_general(train_every, weighted_cotan, contract_rows, preferred_ele...  8.79 us
    unnamed x10, local copies, waits for them, and re-layouts  8.21 us
  transfers between devices with their start and end apart: 4, of which 3 were waited for; matrix products, arithmetic and copies ran while one was open for 4% of the time, Pallas kernels for 0%

commit v1 on v0

--- a/solution.py
+++ b/solution.py
@@ -46,7 +46,9 @@
     part_align = jnp.dot(token_part, member, precision=lax.Precision.HIGHEST)
     count_local = val_count[0].astype(jnp.float32)
     val_total = lax.psum(count_local, ("dp", "sub"))
-    align = lax.psum(part_align, ("dp", "tensor", "sub"))
+    align = part_align
+    for over in (("tensor", "sub"), "dp"):
+        align = lax.psum(align, over)
     lengths = seq_len.astype(jnp.float32)
     score = align / jnp.sqrt(val_total * lengths * float(FF) * float(D))
     seq_weight = jax.nn.sigmoid(score)

time: 232 us -> 204 us (0.88)
  waiting for transfers between devices: 123 us -> 102 us
  blocking collectives: 45 us -> 38.3 us
    all_to_all x1, waiting for transfers between devices: 13.4 us -> 0.01 us  [shards(): lax.all_to_all(val_cotan, ('dp', 'sub'), split_axis=1, concat_axis=0, til...]
    psum x1 -> x2, blocking collectives: 29.9 us -> 16.6 us  [shards(): align = lax.psum(align, over)]
    all_gather x1, waiting for transfers between devices: 57.7 us -> 49.5 us  [shards(): lax.all_gather(train_hidden, ('dp', 'sub'), axis=0, tiled=True)]
    psum x1, blocking collectives: 15.1 us -> 21.7 us  [shards(): val_total = lax.psum(count_local, ('dp', 'sub'))]
  transfers between devices with their start and end apart: 4 -> 4, of which waited for: 3 -> 2; matrix products, arithmetic and copies ran while one was open for 4% -> 4% of each run, Pallas kernels for 0% -> 0%
where the time goes in v1:
time: 204 us
  waiting for transfers between devices  102 us (50%)
  blocking collectives  38.3 us (19%)
  matrix products  20.5 us (10%)
  between operations  15.5 us (8%)
  local copies, waits for them, and re-layouts  12.9 us (6%)
  starting transfers between devices  9.9 us (5%)
  other arithmetic  4.82 us (2%)
    all_to_all x1, waiting for transfers between devices, shards(): lax.all_to_all(train_cotan, ('dp', 'sub'), split_axis=1, concat_axis=0, t...  51.4 us
    all_gather x1, waiting for transfers between devices, shards(): lax.all_gather(train_hidden, ('dp', 'sub'), axis=0, tiled=True)  49.5 us
    psum x1, blocking collectives, shards(): val_total = lax.psum(count_local, ('dp', 'sub'))  21.7 us
    psum x2, blocking collectives, shards(): align = lax.psum(align, over)  16.6 us
    dot_general x1, matrix products, shards(): jnp.dot(train_every, val_grad, preferred_element_type=jnp.float32)  10.6 us
    dot_general x1, matrix products, shards(): lax.dot_general(train_every, weighted_cotan, contract_rows, preferred_ele...  8.78 us
    unnamed x10, local copies, waits for them, and re-layouts  8.21 us
    all_to_all x1, starting transfers between devices, shards(): lax.all_to_all(train_cotan, ('dp', 'sub'), split_axis=1, concat_axis=0, t...  6.33 us
  transfers between devices with their start and end apart: 4, of which 2 were waited for; matrix products, arithmetic and copies ran while one was open for 4% of the time, Pallas kernels for 0%

profile of v1, /device:TPU:0, one launch (start us, length us, event | category | flops | bytes accessed | tf_op | source)
XLA Modules:
  0.0 203.5 jit_solution(12670689197034346567)
XLA Ops:
  7.2 0.0 copy-start
  7.2 0.0 all-gather.3.cloned.1.call-start
  7.9 1.9 broadcast_select_fusion
  9.8 0.0 all-gather.3.cloned.1.call-update
  9.8 0.0 copy-start.1
  9.9 0.0 copy-start.2
  9.9 0.0 all-gather.5.cloned.1.call-start
  9.9 0.7 all-gather.5.cloned.1.call-update
  10.6 2.3 %copy.22 = bf16[128,4096]{0,1:T(8,128)(2,1)} copy(bf16[128,4096]{1,0:T(8,128)(2,1)} %param.11) | data formatting | bytes 2097152 | tf_op args[4]
  12.9 6.3 %all-to-all-start.1 = ((bf16[128,8,512]{0,2,1:T(8,128)(2,1)}), bf16[128,8,512]{0,2,1:T(8,128)(2,1)S(1)}, u32[]{:S(2)}, u32[]{:S(2)}) async-start(bf16[128,8,512]{0,2,1:T(8,128)(2,1)} %bitcast.4), calls=%async_computation.1 | async-start | bytes 2097152 | tf_op jit(solution)/shard_map/all_to_all | solution.py:33
  19.2 0.0 copy-done
  19.2 0.9 copy.28
  20.1 51.4 %all-to-all-done.1 = bf16[128,8,512]{0,2,1:T(8,128)(2,1)S(1)} async-done(((bf16[128,8,512]{0,2,1:T(8,128)(2,1)}), bf16[128,8,512]{0,2,1:T(8,128)(2,1)S(1)}, u32[]{:S(2)}, u32[]{:S(2)}) %all-to-all-start.1) | async-done | bytes 1048608 | tf_op jit(solution)/shard_map/all_to_all | solution.py:33
  71.5 3.5 %all-to-all-start = ((bf16[64,8,512]{2,0,1:T(8,128)(2,1)}), bf16[64,8,512]{2,0,1:T(8,128)(2,1)S(1)}, u32[]{:S(2)}, u32[]{:S(2)}) async-start(bf16[64,8,512]{2,0,1:T(8,128)(2,1)} %bitcast.29), calls=%async_computation | async-start | bytes 1048576 | tf_op jit(solution)/shard_map/all_to_all | solution.py:32
  75.0 21.7 %psum.23 = f32[]{:T(128)} all-reduce(f32[]{:T(128)S(6)} %convert_element_type.33), channel_id=1, replica_groups=mesh['groups'=2,'dp'=4,'tensor'=2,'sub'=2] {'dp','sub'}, use_global_device_ids=true, to_apply=%region_4.5 | all-reduce | flops 1 | bytes 8 | tf_op jit(solution)/shard_map/psum | solution.py:48
  96.7 0.0 copy-done.1
  96.7 0.0 copy-done.2
  96.7 0.2 select_reduce_fusion
  96.9 1.5 convert_bitcast_fusion
  98.4 2.0 copy.23
  100.4 1.8 copy.24
  102.2 0.0 all-to-all-done
  102.2 49.5 %all-gather.5.cloned.1.call-done = bf16[1024,3584]{1,0:T(8,128)(2,1)} async-done(((bf16[128,3584]{1,0:T(8,128)(2,1)}), bf16[1024,3584]{1,0:T(8,128)(2,1)}) %all-gather.5.cloned.1.call-update) | async-done | bytes 7340048 | tf_op jit(solution)/shard_map/all_gather | solution.py:37
  151.7 10.6 %fusion.1 = f32[1024]{0:T(1024)S(1)} fusion(f32[1024,512]{0,1:T(8,128)} %copy.24, bf16[1024,3584]{1,0:T(8,128)(2,1)} %all-gather.5.cloned.1.call-done, bf16[512,3584]{1,0:T(8,128)(2,1)} %all-gather.3.cloned.1.call-done, bf16[512,512]{1,0:T(8,128)(2,1)S(1)} %bitcast.35), kind=kOutput, calls=%fused_computation.4 | convolution fusion | flops 5640027136 | bytes 13635584 | tf_op jit(solution)/shard_map/dot_general | solution.py:43
  162.3 0.5 convolution_bitcast_fusion
  162.9 7.0 %psum.21 = f32[16]{0:T(128)S(1)} all-reduce(f32[16]{0:T(128)S(1)} %convolution_bitcast_fusion), channel_id=1, replica_groups=mesh['groups'=2,'dp'=4,'tensor'=2,'sub'=2] {'tensor','sub'}, use_global_device_ids=true, to_apply=%region_2.3 | all-reduce | flops 16 | bytes 128 | tf_op jit(solution)/shard_map/psum | solution.py:51
  169.9 9.6 %psum.22 = f32[16]{0:T(128)S(1)} all-reduce(f32[16]{0:T(128)S(1)} %psum.21), channel_id=1, replica_groups=mesh['groups'=2,'dp'=4,'tensor'=2,'sub'=2] {'dp'}, use_global_device_ids=true, to_apply=%region_3.4 | all-reduce | flops 16 | bytes 128 | tf_op jit(solution)/shard_map/psum | solution.py:51
  179.4 1.3 multiply_reduce_fusion
  181.4 0.6 fusion.3
  182.0 8.8 %fusion = bf16[3584,512]{0,1:T(8,128)(2,1)} fusion(bf16[1024,3584]{1,0:T(8,128)(2,1)} %all-gather.5.cloned.1.call-done, f32[]{:T(128)S(6)} %sqrt.7, f32[1024,512]{1,0:T(8,128)S(1)} %bitcast.33, f32[1024]{0:T(1024)S(1)} %bitcast.36), kind=kOutput, calls=%fused_computation.2 | convolution fusion | flops 3762814976 | bytes 13111300 | tf_op jit(solution)/shard_map/dot_general | solution.py:58
  190.7 0.0 copy-done.3
  190.7 5.9 %copy.25 = bf16[3584,512]{1,0:T(8,128)(2,1)} copy(bf16[3584,512]{0,1:T(8,128)(2,1)} %fusion) | data formatting | bytes 7340032
  (5 shorter events, 0.0 us)
Async XLA Ops:
  7.2 12.1 %copy-start = (bf16[64,4096]{1,0:T(8,128)(2,1)S(1)}, bf16[64,4096]{1,0:T(8,128)(2,1)}, u32[]{:S(2)}) copy-start(bf16[64,4096]{1,0:T(8,128)(2,1)} %param.8) | copy-start | bytes 1572868
  7.2 95.0 %all-gather.3.cloned.1.call-start = ((), (), s32[]{:S(2)}) async-start(), calls=%async_computation.2 | async-start | bytes 4128768 | tf_op jit(solution)/shard_map/all_gather | solution.py:36
  9.8 86.9 %copy-start.1 = (s32[16]{0:T(128)S(1)}, s32[16]{0:T(128)}, u32[]{:S(2)}) copy-start(s32[16]{0:T(128)} %param.12) | copy-start | bytes 196
  9.9 86.9 %copy-start.2 = (s32[16]{0:T(128)S(1)}, s32[16]{0:T(128)}, u32[]{:S(2)}) copy-start(s32[16]{0:T(128)} %param.13) | copy-start | bytes 196
  9.9 141.8 %all-gather.5.cloned.1.call-start = ((), (), s32[]{:S(2)}) async-start(), calls=%async_computation.3 | async-start | bytes 8257536 | tf_op jit(solution)/shard_map/all_gather | solution.py:37
  12.9 58.6 %all-to-all-start.1 = ((bf16[128,8,512]{0,2,1:T(8,128)(2,1)}), bf16[128,8,512]{0,2,1:T(8,128)(2,1)S(1)}, u32[]{:S(2)}, u32[]{:S(2)}) async-start(bf16[128,8,512]{0,2,1:T(8,128)(2,1)} %bitcast.4), calls=%async_computation.1 | async-start | bytes 2097152 | tf_op jit(solution)/shard_map/all_to_all | solution.py:33
  71.5 30.7 %all-to-all-start = ((bf16[64,8,512]{2,0,1:T(8,128)(2,1)}), bf16[64,8,512]{2,0,1:T(8,128)(2,1)S(1)}, u32[]{:S(2)}, u32[]{:S(2)}) async-start(bf16[64,8,512]{2,0,1:T(8,128)(2,1)} %bitcast.29), calls=%async_computation | async-start | bytes 1048576 | tf_op jit(solution)/shard_map/all_to_all | solution.py:32
  180.7 10.1 %copy-start.3 = (f32[16]{0:T(128)}, f32[16]{0:T(128)S(1)}, u32[]{:S(2)}) copy-start(f32[16]{0:T(128)S(1)} %get-tuple-element.13) | copy-start | bytes 196
Sparse Core Ops, SparseCore 0:
  10.0 66.9 all-gather.2
  78.6 73.0 all-gather.4
